TPU v7x, 512 devices: a whole 4x8x8 slice. The times are simulated.
512 devices in a mesh: ctx: 128 (over y_hi, z, x, core), tp: 4 (over y_lo).
Axes of the slice: x: 4, y: 8 (y_hi: 2, y_lo: 4; y = y_hi * 4 + y_lo), z: 8, core: 2. Of those that a mesh axis runs over, the one named last changes fastest.
Arguments:
- streams: bfloat16 [3, 4096, 16384], P(None, 'tp', 'ctx'), may hold values from -6 to 6
- conv_weight: float32 [3, 7, 4096], P(None, None, 'tp'), may hold values from -2 to 2
- rates: float32 [512, 16], P('tp'), may hold values from 1.2207031e-05 to 0.05
- residues: float32 [512, 16], P('tp'), may hold values from -4 to 4
- skip: float32 [4096], P('tp'), may hold values from -4 to 4
- out_weight: bfloat16 [4096, 4096], P('ctx', 'tp'), may hold values from -0.09375 to 0.09375
Outputs:
- result: bfloat16 [16384, 4096], P('ctx', 'tp')
All inputs are finite; a program needn't handle non-finite values.
Results may differ from a plain program's by a relative error of at most 0.014.
Values may be sent and summed in bfloat16 or wider, within the bound.
A program may use at most 128 MiB of HBM per device.

v0:
```python
import math
import jax
import jax.numpy as jnp
from jax import lax
from jax.sharding import PartitionSpec as P


def from_behind(value, axis, steps):
    count = lax.axis_size(axis)
    leading, last = (max(0, -steps), min(count, count - steps))
    return lax.ppermute(value, axis, [(source, source + steps) for source in range(leading, last)])


def block_parts(signal, coefficient, rates):
    groups = coefficient.shape[0]
    channels, length = signal.shape
    group_width = channels // groups
    block_len = 128
    block_count = length // block_len
    blocks = signal.reshape(groups, group_width, block_count, block_len)
    position = jnp.arange(block_len, dtype=jnp.float32)
    centre = (block_len - 1.0) * 0.5
    left_factor = coefficient[:, :, None] * jnp.exp(-rates[:, :, None] * (position - centre))
    right_factor = jnp.exp(rates[:, :, None] * (position - centre))
    causal = (position[:, None] >= position[None, :]).astype(jnp.float32)
    toeplitz = (
        jnp.einsum("gni,gnj->gij", left_factor, right_factor, precision=lax.Precision.HIGHEST)
        * causal
    )
    inside = jnp.einsum("gij,gcbj->gcbi", toeplitz, blocks, precision=lax.Precision.HIGHEST)
    tail_decay = jnp.exp(-rates[:, :, None] * (block_len - 1.0 - position))
    block_ends = jnp.einsum("gnj,gcbj->gcbn", tail_decay, blocks, precision=lax.Precision.HIGHEST)
    block_index = jnp.arange(block_count, dtype=jnp.float32)
    lag = block_index[:, None] - block_index[None, :]
    earlier_mask = (lag >= 1.0).astype(jnp.float32)
    steps_back = jnp.maximum(lag - 1.0, 0.0)
    carry_matrix = jnp.exp(-rates[:, :, None, None] * block_len * steps_back) * earlier_mask
    entering = jnp.einsum(
        "gnab,gcbn->gcan", carry_matrix, block_ends, precision=lax.Precision.HIGHEST
    )
    last_decay = jnp.exp(-rates[:, :, None] * block_len * (block_count - 1.0 - block_index))
    segment_end = jnp.einsum(
        "gnb,gcbn->gcn", last_decay, block_ends, precision=lax.Precision.HIGHEST
    )
    return (inside, entering, segment_end)


def finish_conv(inside, entering, coefficient, rates):
    groups, group_width, block_count, block_len = inside.shape
    position = jnp.arange(block_len, dtype=jnp.float32)
    lift_out = coefficient[:, :, None] * jnp.exp(-rates[:, :, None] * (position + 1.0))
    total = inside + jnp.einsum(
        "gni,gcbn->gcbi", lift_out, entering, precision=lax.Precision.HIGHEST
    )
    return total.reshape(groups * group_width, block_count * block_len)


def local(streams, conv_weight, rates, residues, skip, out_weight):
    tap_count = conv_weight.shape[1]
    rim_width = tap_count - 1
    length = streams.shape[2]
    tail_rows = jnp.swapaxes(streams[:, :, length - rim_width :], 1, 2)
    before = from_behind(tail_rows, "ctx", 1)
    extended = jnp.concatenate([jnp.swapaxes(before, 1, 2), streams], axis=2)
    filtered = conv_weight[:, 0, :, None] * extended[:, :, rim_width:].astype(jnp.float32)
    for shift_by in range(1, tap_count):
        filtered = filtered + conv_weight[:, shift_by, :, None] * extended[
            :, :, rim_width - shift_by : rim_width - shift_by + length
        ].astype(jnp.float32)
    queries = filtered[0]
    gated_in = (filtered[1] * filtered[2]).astype(jnp.bfloat16)
    gated_wide = gated_in.astype(jnp.float32)
    coefficient = residues * jnp.sqrt(2.0 * rates) / math.sqrt(rates.shape[1])
    by_channel = lax.all_to_all(gated_in, "ctx", split_axis=0, concat_axis=1, tiled=True)
    per_device = rates.shape[0] // lax.axis_size("ctx")
    first_group = lax.axis_index("ctx") * per_device
    coef_mine = lax.dynamic_slice_in_dim(coefficient, first_group, per_device, 0)
    rates_mine = lax.dynamic_slice_in_dim(rates, first_group, per_device, 0)
    inside, entering, segment_end = block_parts(
        by_channel.astype(jnp.float32), coef_mine, rates_mine
    )
    filtered_all = finish_conv(inside, entering, coef_mine, rates_mine)
    conv_out = lax.all_to_all(filtered_all, "ctx", split_axis=1, concat_axis=0, tiled=True)
    mixed_out = (queries * (conv_out + skip[:, None] * gated_wide)).astype(jnp.bfloat16)
    features = lax.all_gather(mixed_out, "tp", axis=0, tiled=True)
    summed = lax.dot_general(
        features,
        lax.all_gather(out_weight, "ctx", axis=0, tiled=True),
        (((0,), (0,)), ((), ())),
        preferred_element_type=jnp.float32,
    )
    return summed.astype(jnp.bfloat16)


def solution(mesh):
    return jax.shard_map(
        local,
        mesh=mesh,
        in_specs=(
            P(None, "tp", "ctx"),
            P(None, None, "tp"),
            P("tp", None),
            P("tp", None),
            P("tp"),
            P("ctx", "tp"),
        ),
        out_specs=P("ctx", "tp"),
        check_vma=False,
    )
```

profile of v0, /device:TPU:1, one launch (start us, length us, event | category | flops | bytes accessed | tf_op | source)
XLA Modules:
  0.0 293.7 jit_solution(14990521191751933927)
XLA Ops:
  6.5 0.0 copy-start.1
  6.5 0.0 copy-start.3
  6.5 0.0 copy-start.2
  6.5 0.0 copy-start
  6.5 1.5 slice.53
  8.0 0.3 copy.24
  8.3 4.5 %collective-permute-start = (bf16[3,6,1024]{2,1,0:T(8,128)(2,1)S(1)}, bf16[3,6,1024]{2,1,0:T(8,128)(2,1)S(1)}, u32[]{:S(2)}, u32[]{:S(2)}) collective-permute-start(bf16[3,6,1024]{2,1,0:T(8,128)(2,1)S(1)} %bitcast.64), channel_id=1, source_target_pairs={{0,4},{4,8},{8,12},{12,16},{16,20},{20,24},{24,28},{28,32},{32,36}... | collective-permute-start | bytes 110600 | tf_op jit(solution)/shard_map/ppermute | solution.py:11
  12.9 0.0 copy-done.1
  12.9 0.1 fusion.51
  13.1 0.0 copy-done.3
  13.1 0.0 copy-done.2
  13.1 0.2 fusion.27
  13.3 3.9 %collective-permute-done = bf16[3,6,1024]{2,1,0:T(8,128)(2,1)S(1)} collective-permute-done((bf16[3,6,1024]{2,1,0:T(8,128)(2,1)S(1)}, bf16[3,6,1024]{2,1,0:T(8,128)(2,1)S(1)}, u32[]{:S(2)}, u32[]{:S(2)}) %collective-permute-start) | collective-permute-done | bytes 36896 | tf_op jit(solution)/shard_map/ppermute | solution.py:11
  17.2 0.4 copy.12
  17.6 0.0 copy-done
  17.6 5.6 %multiply_add_fusion = f32[3,1024,128]{2,1,0:T(8,128)S(1)} fusion(bf16[3,1024,128]{2,1,0:T(8,128)(2,1)S(1)} %copy-done, bf16[3,1024,6]{2,1,0:T(8,128)(2,1)S(1)} %bitcast.62, f32[3,1024]{1,0:T(4,128)S(1)} %get-tuple-element.16, f32[3,1024]{1,0:T(4,128)S(1)} %get-tuple-element.17, f32[3,1024]{1,0:T(4,128)S(1)} %get-tuple-element.18, ...), kind=kLoop, calls=%fused_computation.10 | loop fusion | flops 14942208 | bytes 2482176 | tf_op jit(solution)/shard_map/add | solution.py:67
  23.2 0.8 fusion.55
  24.0 18.2 %all-to-all-start = ((bf16[128,8,128]{2,1,0:T(8,128)(2,1)}), bf16[128,8,128]{2,1,0:T(8,128)(2,1)S(1)}, u32[]{:S(2)}, u32[]{:S(2)}) async-start(bf16[128,8,128]{2,1,0:T(8,128)(2,1)} %fusion.55), calls=%async_computation | async-start | bytes 524288 | tf_op jit(solution)/shard_map/all_to_all | solution.py:74
  42.2 0.0 all-gather.3.cloned.1.call-start
  42.3 0.4 fusion
  42.7 17.0 %all-to-all-done = bf16[128,8,128]{2,1,0:T(8,128)(2,1)S(1)} async-done(((bf16[128,8,128]{2,1,0:T(8,128)(2,1)}), bf16[128,8,128]{2,1,0:T(8,128)(2,1)S(1)}, u32[]{:S(2)}, u32[]{:S(2)}) %all-to-all-start) | async-done | bytes 262176 | tf_op jit(solution)/shard_map/all_to_all | solution.py:74
  59.7 0.3 fusion.16
  60.0 1.9 convolution_bitcast_fusion
  61.9 0.4 fusion.18
  62.3 0.0 copy-start.4
  62.3 1.0 convolution_add_fusion
  63.3 0.3 copy.16
  63.6 29.5 %all_to_all.29 = f32[8,128,128]{2,0,1:T(8,128)S(1)} all-to-all(f32[8,128,128]{2,0,1:T(8,128)S(1)} %copy.16), channel_id=1, replica_groups=mesh['ctx'=128,'tp'=4] {'ctx'}, dimensions={1} | all-to-all | bytes 1048576 | tf_op jit(solution)/shard_map/all_to_all | solution.py:83
  93.1 0.0 copy-done.4
  93.1 0.9 fusion.11
  94.0 0.0 all-gather.3.cloned.1.call-update
  94.0 0.0 all-gather.5.cloned.1.call-start
  94.1 0.7 all-gather.5.cloned.1.call-update
  94.8 26.1 %all-gather.3.cloned.1.call-done = bf16[4096,128]{1,0:T(8,128)(2,1)} async-done(((bf16[1024,128]{1,0:T(8,128)(2,1)}), bf16[4096,128]{1,0:T(8,128)(2,1)}) %all-gather.3.cloned.1.call-update) | async-done | bytes 1048592 | tf_op jit(solution)/shard_map/all_gather | solution.py:85
  120.9 160.3 %all-gather.5.cloned.1.call-done = bf16[4096,1024]{1,0:T(8,128)(2,1)} async-done(((bf16[32,1024]{1,0:T(8,128)(2,1)}), bf16[4096,1024]{1,0:T(8,128)(2,1)}) %all-gather.5.cloned.1.call-update) | async-done | bytes 8388624 | tf_op jit(solution)/shard_map/all_gather | solution.py:88
  281.2 5.7 %convolution_convert_fusion = bf16[128,1024]{1,0:T(8,128)(2,1)} fusion(bf16[4096,128]{1,0:T(8,128)(2,1)} %all-gather.3.cloned.1.call-done, bf16[4096,1024]{1,0:T(8,128)(2,1)} %all-gather.5.cloned.1.call-done), kind=kOutput, calls=%fused_computation.12 | convolution fusion | flops 1073872896 | bytes 9699328 | tf_op jit(solution)/shard_map/dot_general | solution.py:86
  (10 shorter events, 0.1 us)
Async XLA Ops:
  6.5 6.4 %copy-start.1 = (f32[3,7,1024]{2,1,0:T(8,128)S(1)}, f32[3,7,1024]{2,1,0:T(8,128)}, u32[]{:S(2)}) copy-start(f32[3,7,1024]{2,1,0:T(8,128)} %param.7) | copy-start | bytes 258052
  6.5 6.5 %copy-start.3 = (f32[128,16]{0,1:T(8,128)S(1)}, f32[128,16]{0,1:T(8,128)}, u32[]{:S(2)}) copy-start(f32[128,16]{0,1:T(8,128)} %param.8) | copy-start | bytes 24580
  6.5 6.5 %copy-start.2 = (f32[128,16]{0,1:T(8,128)S(1)}, f32[128,16]{0,1:T(8,128)}, u32[]{:S(2)}) copy-start(f32[128,16]{0,1:T(8,128)} %param.9) | copy-start | bytes 24580
  6.5 11.1 %copy-start = (bf16[3,1024,128]{2,1,0:T(8,128)(2,1)S(1)}, bf16[3,1024,128]{2,1,0:T(8,128)(2,1)}, u32[]{:S(2)}) copy-start(bf16[3,1024,128]{2,1,0:T(8,128)(2,1)} %param.6) | copy-start | bytes 2359300
  8.3 8.9 %collective-permute-start = (bf16[3,6,1024]{2,1,0:T(8,128)(2,1)S(1)}, bf16[3,6,1024]{2,1,0:T(8,128)(2,1)S(1)}, u32[]{:S(2)}, u32[]{:S(2)}) collective-permute-start(bf16[3,6,1024]{2,1,0:T(8,128)(2,1)S(1)} %bitcast.64), channel_id=1, source_target_pairs={{0,4},{4,8},{8,12},{12,16},{16,20},{20,24},{24,28},{28,32},{32,36}... | collective-permute-start | bytes 110600 | tf_op jit(solution)/shard_map/ppermute | solution.py:11
  24.0 35.7 %all-to-all-start = ((bf16[128,8,128]{2,1,0:T(8,128)(2,1)}), bf16[128,8,128]{2,1,0:T(8,128)(2,1)S(1)}, u32[]{:S(2)}, u32[]{:S(2)}) async-start(bf16[128,8,128]{2,1,0:T(8,128)(2,1)} %fusion.55), calls=%async_computation | async-start | bytes 524288 | tf_op jit(solution)/shard_map/all_to_all | solution.py:74
  42.2 78.7 %all-gather.3.cloned.1.call-start = ((), (), s32[]{:S(2)}) async-start(), calls=%async_computation.2 | async-start | bytes 1310720 | tf_op jit(solution)/shard_map/all_gather | solution.py:85
  62.3 30.8 %copy-start.4 = (f32[1024]{0:T(1024)S(1)}, f32[1024]{0:T(1024)}, u32[]{:S(2)}) copy-start(f32[1024]{0:T(1024)} %param.10) | copy-start | bytes 12292
  94.0 187.2 %all-gather.5.cloned.1.call-start = ((), (), s32[]{:S(2)}) async-start(), calls=%async_computation.3 | async-start | bytes 8454144 | tf_op jit(solution)/shard_map/all_gather | solution.py:88
Sparse Core Ops, SparseCore 0:
  94.1 26.7 all-gather.2
  125.5 155.6 all-gather.4
where the time goes:
time: 294 us
  waiting for transfers between devices  208 us (71%)
  blocking collectives  29.5 us (10%)
  starting transfers between devices  22.8 us (8%)
  between operations  13.6 us (5%)
  matrix products  9.69 us (3%)
  other arithmetic  7.52 us (3%)
    all_gather x1, waiting for transfers between devices, local(): lax.all_gather(out_weight, 'ctx', axis=0, tiled=True)  160 us
    all_to_all x1, blocking collectives, local(): lax.all_to_all(filtered_all, 'ctx', split_axis=1, concat_axis=0, tiled=True)  29.5 us
    all_gather x1, waiting for transfers between devices, local(): features = lax.all_gather(mixed_out, 'tp', axis=0, tiled=True)  26.1 us
    all_to_all x1, starting transfers between devices, local(): lax.all_to_all(gated_in, 'ctx', split_axis=0, concat_axis=1, tiled=True)  18.2 us
    all_to_all x1, waiting for transfers between devices, local(): lax.all_to_all(gated_in, 'ctx', split_axis=0, concat_axis=1, tiled=True)  17 us
  transfers between devices with their start and end apart: 4, of which 4 were waited for; matrix products, arithmetic and copies ran while one was open for 0% of the time, Pallas kernels for 0%

commit v1 on v0

--- a/solution.py
+++ b/solution.py
@@ -85,7 +85,9 @@
     features = lax.all_gather(mixed_out, "tp", axis=0, tiled=True)
     summed = lax.dot_general(
         features,
-        lax.all_gather(out_weight, "ctx", axis=0, tiled=True),
+        jnp.concatenate(
+            lax.all_to_all(jnp.stack([out_weight] * lax.axis_size("ctx")), "ctx", 0, 0), axis=0
+        ),
         (((0,), (0,)), ((), ())),
         preferred_element_type=jnp.float32,
     )

time: 294 us -> 364 us (1.24)
  the two profiles are of different devices: /device:TPU:1 before, /device:TPU:16 now
where the time goes in v1:
time: 364 us; the launch traced here: 363 us
  waiting for transfers between devices  265 us (73%)
  starting transfers between devices  31.5 us (9%)
  blocking collectives  29.4 us (8%)
  between operations  13.6 us (4%)
  matrix products  9.68 us (3%)
  other arithmetic  7.52 us (2%)
  local copies, waits for them, and re-layouts  6.96 us (2%)
    all_to_all x1, waiting for transfers between devices, local(): lax.all_to_all(jnp.stack([out_weight] * lax.axis_size('ctx')), 'ctx', 0, 0)  174 us
    all_gather x1, waiting for transfers between devices, local(): features = lax.all_gather(mixed_out, 'tp', axis=0, tiled=True)  71.8 us
    all_to_all x1, blocking collectives, local(): lax.all_to_all(filtered_all, 'ctx', split_axis=1, concat_axis=0, tiled=True)  29.4 us
    all_to_all x1, starting transfers between devices, local(): lax.all_to_all(gated_in, 'ctx', split_axis=0, concat_axis=1, tiled=True)  22.1 us
    all_to_all x1, waiting for transfers between devices, local(): lax.all_to_all(gated_in, 'ctx', split_axis=0, concat_axis=1, tiled=True)  18 us
    all_to_all x1, starting transfers between devices, local(): lax.all_to_all(jnp.stack([out_weight] * lax.axis_size('ctx')), 'ctx', 0, 0)  7.62 us
  transfers between devices with their start and end apart: 4, of which 4 were waited for; matrix products, arithmetic and copies ran while one was open for 0% of the time, Pallas kernels for 0%

profile of v1, /device:TPU:16, one launch (start us, length us, event | category | flops | bytes accessed | tf_op | source)
XLA Modules:
  0.0 363.2 jit_solution(1777210372457659669)
XLA Ops:
  6.5 0.0 copy-start
  6.5 0.0 copy-start.1
  6.5 0.0 copy-start.3
  6.5 0.0 copy-start.4
  6.5 1.5 slice.53
  8.0 0.3 copy.24
  8.3 1.7 collective-permute-start
  10.1 0.0 copy-done.1
  10.1 0.1 fusion.51
  10.3 0.0 copy-done.3
  10.3 0.0 copy-done.4
  10.3 0.2 fusion.27
  10.5 0.4 collective-permute-done
  10.9 0.4 copy.12
  11.4 0.0 copy-done
  11.4 5.6 %multiply_add_fusion = f32[3,1024,128]{2,1,0:T(8,128)S(1)} fusion(bf16[3,1024,128]{2,1,0:T(8,128)(2,1)S(1)} %copy-done, bf16[3,1024,6]{2,1,0:T(8,128)(2,1)S(1)} %bitcast.63, f32[3,1024]{1,0:T(4,128)S(1)} %get-tuple-element.16, f32[3,1024]{1,0:T(4,128)S(1)} %get-tuple-element.17, f32[3,1024]{1,0:T(4,128)S(1)} %get-tuple-element.18, ...), kind=kLoop, calls=%fused_computation.10 | loop fusion | flops 14942208 | bytes 2482176 | tf_op jit(solution)/shard_map/add | solution.py:67
  17.0 0.8 fusion.55
  17.7 22.1 %all-to-all-start = ((bf16[128,8,128]{2,1,0:T(8,128)(2,1)}), bf16[128,8,128]{2,1,0:T(8,128)(2,1)S(1)}, u32[]{:S(2)}, u32[]{:S(2)}) async-start(bf16[128,8,128]{2,1,0:T(8,128)(2,1)} %fusion.55), calls=%async_computation | async-start | bytes 524288 | tf_op jit(solution)/shard_map/all_to_all | solution.py:74
  39.9 0.4 fusion
  40.3 18.0 %all-to-all-done = bf16[128,8,128]{2,1,0:T(8,128)(2,1)S(1)} async-done(((bf16[128,8,128]{2,1,0:T(8,128)(2,1)}), bf16[128,8,128]{2,1,0:T(8,128)(2,1)S(1)}, u32[]{:S(2)}, u32[]{:S(2)}) %all-to-all-start) | async-done | bytes 262176 | tf_op jit(solution)/shard_map/all_to_all | solution.py:74
  58.2 0.3 fusion.16
  58.6 1.9 convolution_bitcast_fusion
  60.4 0.4 fusion.18
  60.8 0.0 copy-start.2
  60.8 1.0 convolution_add_fusion
  61.9 0.3 copy.16
  62.2 29.4 %all_to_all.34 = f32[8,128,128]{2,0,1:T(8,128)S(1)} all-to-all(f32[8,128,128]{2,0,1:T(8,128)S(1)} %copy.16), channel_id=1, replica_groups=mesh['ctx'=128,'tp'=4] {'ctx'}, dimensions={1} | all-to-all | bytes 1048576 | tf_op jit(solution)/shard_map/all_to_all | solution.py:83
  91.6 0.0 copy-done.2
  91.6 4.3 %stack.2 = bf16[128,32,1024]{2,1,0:T(8,128)(2,1)} broadcast(bf16[32,1024]{1,0:T(8,128)(2,1)S(1)} %copy-done.2), dimensions={1,2} | broadcast | bytes 8454144 | tf_op jit(solution)/shard_map/stack | solution.py:89
  95.9 0.0 copy-start.5
  95.9 7.6 %all-to-all-start.2 = ((bf16[128,32,1024]{2,1,0:T(8,128)(2,1)}), bf16[128,32,1024]{2,1,0:T(8,128)(2,1)}, u32[]{:S(2)}, u32[]{:S(2)}) async-start(bf16[128,32,1024]{2,1,0:T(8,128)(2,1)} %stack.2), calls=%async_computation.2 | async-start | bytes 16777216 | tf_op jit(solution)/shard_map/all_to_all | solution.py:89
  103.5 0.0 all-gather.2.cloned.1.call-start
  103.6 0.0 copy-done.5
  103.6 0.9 fusion.11
  104.5 0.0 all-gather.2.cloned.1.call-update
  104.5 71.8 %all-gather.2.cloned.1.call-done = bf16[4096,128]{1,0:T(8,128)(2,1)} async-done(((bf16[1024,128]{1,0:T(8,128)(2,1)}), bf16[4096,128]{1,0:T(8,128)(2,1)}) %all-gather.2.cloned.1.call-update) | async-done | bytes 1048592 | tf_op jit(solution)/shard_map/all_gather | solution.py:85
  176.3 174.3 %all-to-all-done.2 = bf16[128,32,1024]{2,1,0:T(8,128)(2,1)} async-done(((bf16[128,32,1024]{2,1,0:T(8,128)(2,1)}), bf16[128,32,1024]{2,1,0:T(8,128)(2,1)}, u32[]{:S(2)}, u32[]{:S(2)}) %all-to-all-start.2) | async-done | bytes 8388640 | tf_op jit(solution)/shard_map/all_to_all | solution.py:89
  350.6 5.7 %convolution_convert_fusion = bf16[128,1024]{1,0:T(8,128)(2,1)} fusion(bf16[4096,128]{1,0:T(8,128)(2,1)} %all-gather.2.cloned.1.call-done, bf16[4096,1024]{1,0:T(8,128)(2,1)} %bitcast.17), kind=kOutput, calls=%fused_computation.12 | convolution fusion | flops 1073872896 | bytes 9699328 | tf_op jit(solution)/shard_map/dot_general | solution.py:86
  (10 shorter events, 0.1 us)
Async XLA Ops:
  6.5 4.8 %copy-start = (bf16[3,1024,128]{2,1,0:T(8,128)(2,1)S(1)}, bf16[3,1024,128]{2,1,0:T(8,128)(2,1)}, u32[]{:S(2)}) copy-start(bf16[3,1024,128]{2,1,0:T(8,128)(2,1)} %param.6) | copy-start | bytes 2359300
  6.5 3.6 copy-start.1
  6.5 3.8 %copy-start.3 = (f32[128,16]{0,1:T(8,128)S(1)}, f32[128,16]{0,1:T(8,128)}, u32[]{:S(2)}) copy-start(f32[128,16]{0,1:T(8,128)} %param.9) | copy-start | bytes 24580
  6.5 3.8 %copy-start.4 = (f32[128,16]{0,1:T(8,128)S(1)}, f32[128,16]{0,1:T(8,128)}, u32[]{:S(2)}) copy-start(f32[128,16]{0,1:T(8,128)} %param.8) | copy-start | bytes 24580
  8.3 2.6 collective-permute-start
  17.7 40.5 %all-to-all-start = ((bf16[128,8,128]{2,1,0:T(8,128)(2,1)}), bf16[128,8,128]{2,1,0:T(8,128)(2,1)S(1)}, u32[]{:S(2)}, u32[]{:S(2)}) async-start(bf16[128,8,128]{2,1,0:T(8,128)(2,1)} %fusion.55), calls=%async_computation | async-start | bytes 524288 | tf_op jit(solution)/shard_map/all_to_all | solution.py:74
  60.8 30.8 %copy-start.2 = (bf16[32,1024]{1,0:T(8,128)(2,1)S(1)}, bf16[32,1024]{1,0:T(8,128)(2,1)}, u32[]{:S(2)}) copy-start(bf16[32,1024]{1,0:T(8,128)(2,1)} %param.11) | copy-start | bytes 196612
  95.9 7.7 %copy-start.5 = (f32[1024]{0:T(1024)S(1)}, f32[1024]{0:T(1024)}, u32[]{:S(2)}) copy-start(f32[1024]{0:T(1024)} %param.10) | copy-start | bytes 12292
  95.9 254.7 %all-to-all-start.2 = ((bf16[128,32,1024]{2,1,0:T(8,128)(2,1)}), bf16[128,32,1024]{2,1,0:T(8,128)(2,1)}, u32[]{:S(2)}, u32[]{:S(2)}) async-start(bf16[128,32,1024]{2,1,0:T(8,128)(2,1)} %stack.2), calls=%async_computation.2 | async-start | bytes 16777216 | tf_op jit(solution)/shard_map/all_to_all | solution.py:89
  103.5 72.8 %all-gather.2.cloned.1.call-start = ((), (), s32[]{:S(2)}) async-start(), calls=%async_computation.3 | async-start | bytes 1310720 | tf_op jit(solution)/shard_map/all_gather | solution.py:85
Sparse Core Ops, SparseCore 0:
  106.5 69.8 all-gather.1
